TPU v7x, 32 devices: a whole 2x2x4 slice. The times are simulated.
32 devices in a mesh: groups: 2 (over y), rows: 8 (over z, x), tp: 2 (over core).
Axes of the slice: x: 2, y: 2, z: 4, core: 2. Of those that a mesh axis runs over, the one named last changes fastest.
Arguments:
- activations: bfloat16 [2048, 4096], P(('groups', 'rows'), 'tp'), parts along dimension 0, may hold values from -6 to 6
- cotangent: bfloat16 [2048, 16384], P(('groups', 'rows'), 'tp'), parts along dimension 0, may hold values from -0.039794922 to 0.039794922
- adapter_down_factors: bfloat16 [16, 4096, 16], P('rows', 'tp'), may hold values from -1.796875 to 1.796875
- adapter_up_factors: bfloat16 [16, 16384, 16], P('rows', 'tp'), may hold values from -0.8984375 to 0.8984375
- adapter_slot: int32 [16], replicated, may hold values from 0 to 15, each once
- adapter_of_block: int32 [16], P('groups'), parts along dimension 0, may hold values from 0 to 15, as said below
- counts: int32 [32], P('groups'), parts along dimension 0, may hold values from 0 to 512, as said below
Outputs:
- input_grad: bfloat16 [2048, 4096], P(('groups', 'rows'), 'tp'), parts along dimension 0
- grad_down: bfloat16 [32, 4096, 16], P(('groups', 'rows'), 'tp'), parts along dimension 0
- grad_up: bfloat16 [32, 16384, 16], P(('groups', 'rows'), 'tp'), parts along dimension 0
There are 2 independent parts, one for each index of `groups`. A program takes and returns all parts, laid end to end along the dimension named above; an argument that names none is the same for every part. Nothing has to cross between parts.
Inputs may be any that keep to these rules, and one draw needn't show every extreme that they name: `adapter_of_block`: an adapter number; an adapter may own several blocks, and most own none. counts[a] is 0 when no block names adapter a; else it lies between 128 * (n - 1) + 1 and 128 * n, n being the number of blocks that name a; one adapter has exactly 128 * (8 // 2) rows. `adapter_slot`: each slot once.
All inputs are finite; a program needn't handle non-finite values.
Results may differ from a plain program's by a relative error of at most 0.0051.
Values may be sent and summed in bfloat16 or wider, within the bound.
A program may use at most 64 MiB of HBM per device.

v0:
```python
import jax
import jax.numpy as jnp
from jax import lax
from jax.sharding import PartitionSpec as P

BLK = 128


adapter_scale = 2.0


def row_plan(adapter_of_block, counts, adapter_slot):
    labels = jnp.arange(counts.shape[0], dtype=jnp.int32)
    matches = adapter_of_block[:, None] == labels[None, :]
    slot_of_block = jnp.sum(jnp.where(matches, adapter_slot[None, :], 0), axis=1)
    block_count = jnp.sum(jnp.where(matches, counts[None, :], 0), axis=1)
    order = jnp.arange(adapter_of_block.shape[0], dtype=jnp.int32)
    same_adapter = adapter_of_block[:, None] == adapter_of_block[None, :]
    earlier = jnp.sum(jnp.where(same_adapter & (order[None, :] < order[:, None]), 1, 0), axis=1)
    places = jnp.arange(BLK, dtype=jnp.int32)
    active_rows = jnp.where(
        earlier[:, None] * BLK + places[None, :] < block_count[:, None], 1.0, 0.0
    ).astype(jnp.float32)
    return (active_rows, slot_of_block)


def rank_terms(columns, factor_blocks, nblocks):
    pieces = columns.reshape(nblocks, BLK, columns.shape[1])
    return jnp.einsum("btc,bcr->btr", pieces, factor_blocks, preferred_element_type=jnp.float32)


def slot_total(selector, terms, slots):
    flat = terms.reshape(terms.shape[0], -1)
    summed = jnp.dot(
        selector, flat, precision=lax.Precision.HIGHEST, preferred_element_type=jnp.float32
    )
    return summed.reshape(slots, terms.shape[1], terms.shape[2]).astype(jnp.bfloat16)


def on_device(
    activations,
    cotangent,
    adapter_down_factors,
    adapter_up_factors,
    adapter_slot,
    adapter_of_block,
    counts,
):
    nblocks = adapter_of_block.shape[0]
    slots = adapter_slot.shape[0]
    active_rows, slot_of_block = row_plan(adapter_of_block, counts, adapter_slot)
    selector = (slot_of_block[None, :] == jnp.arange(slots, dtype=jnp.int32)[:, None]).astype(
        jnp.float32
    )
    down_cols, up_cols = (
        lax.all_to_all(adapter_down_factors, "rows", split_axis=1, concat_axis=0, tiled=True),
        lax.all_to_all(adapter_up_factors, "rows", split_axis=1, concat_axis=0, tiled=True),
    )
    down_factor_blocks = down_cols[slot_of_block]
    up_factor_blocks = up_cols[slot_of_block]
    input_cols, grad_cols = (
        lax.all_to_all(activations, "rows", split_axis=1, concat_axis=0, tiled=True),
        lax.all_to_all(cotangent, "rows", split_axis=1, concat_axis=0, tiled=True),
    )
    down_sum, up_partial_sum = lax.psum(
        (
            rank_terms(input_cols, down_factor_blocks, nblocks),
            rank_terms(grad_cols, up_factor_blocks, nblocks),
        ),
        ("rows", "tp"),
    )
    reduced_down = (active_rows[:, :, None] * down_sum).astype(jnp.bfloat16)
    reduced_up = (adapter_scale * active_rows[:, :, None] * up_partial_sum).astype(jnp.bfloat16)
    grad_pieces = grad_cols.reshape(nblocks, BLK, grad_cols.shape[1])
    input_pieces = input_cols.reshape(nblocks, BLK, input_cols.shape[1])
    up_contributions = adapter_scale * jnp.einsum(
        "eqi,eqf->eif", grad_pieces, reduced_down, preferred_element_type=jnp.float32
    )
    down_terms = jnp.einsum(
        "eqi,eqf->eif", input_pieces, reduced_up, preferred_element_type=jnp.float32
    )
    grad_up_cols = slot_total(selector, up_contributions, slots)
    grad_down_cols = slot_total(selector, down_terms, slots)
    input_grad_cols = jnp.einsum(
        "btr,bcr->btc", reduced_up, down_factor_blocks, preferred_element_type=jnp.float32
    )
    input_grad_cols = input_grad_cols.reshape(nblocks * BLK, input_cols.shape[1]).astype(
        jnp.bfloat16
    )
    input_grad, grad_down, grad_up = (
        lax.all_to_all(input_grad_cols, "rows", split_axis=0, concat_axis=1, tiled=True),
        lax.all_to_all(grad_down_cols, "rows", split_axis=0, concat_axis=1, tiled=True),
        lax.all_to_all(grad_up_cols, "rows", split_axis=0, concat_axis=1, tiled=True),
    )
    return (input_grad, grad_down, grad_up)


def solution(mesh):
    in_specs = (
        P(("groups", "rows"), "tp"),
        P(("groups", "rows"), "tp"),
        P("rows", "tp", None),
        P("rows", "tp", None),
        P(),
        P("groups"),
        P("groups"),
    )
    out_specs = (
        P(("groups", "rows"), "tp"),
        P(("groups", "rows"), "tp", None),
        P(("groups", "rows"), "tp", None),
    )
    return jax.shard_map(
        on_device, mesh=mesh, in_specs=in_specs, out_specs=out_specs, check_vma=False
    )
```

profile of v0, /device:TPU:0, one launch (start us, length us, event | category | flops | bytes accessed | tf_op | source)
XLA Modules:
  0.0 275.3 jit_solution(13654934744709606557)
XLA Ops:
  11.0 7.3 %all-to-all-start.2 = ((bf16[8,2,4096]{2,1,0:T(2,128)(2,1)}), bf16[8,2,4096]{2,1,0:T(2,128)(2,1)S(1)}, u32[]{:S(2)}, u32[]{:S(2)}) async-start(bf16[8,2,4096]{2,1,0:T(2,128)(2,1)} %reshape.143), calls=%async_computation.2 | async-start | bytes 262144 | tf_op jit(solution)/shard_map/all_to_all | solution.py:56
  18.3 6.7 %copy.58 = bf16[2,8192,16]{2,0,1:T(2,128)(2,1)} copy(bf16[2,8192,16]{1,2,0:T(8,128)(2,1)S(1)} %copy-done) | data formatting | bytes 1048576 | tf_op args[3]
  25.0 6.5 %reshape.145 = bf16[8,2,16384]{2,1,0:T(2,128)(2,1)} reshape(bf16[8192,2,16]{2,1,0:T(2,128)(2,1)} %bitcast.72) | data formatting | bytes 1048576
  31.5 6.0 %all-to-all-start = ((bf16[8,2,16384]{2,1,0:T(2,128)(2,1)}), bf16[8,2,16384]{2,1,0:T(2,128)(2,1)S(1)}, u32[]{:S(2)}, u32[]{:S(2)}) async-start(bf16[8,2,16384]{2,1,0:T(2,128)(2,1)} %reshape.145), calls=%async_computation | async-start | bytes 1048576 | tf_op jit(solution)/shard_map/all_to_all | solution.py:57
  38.8 12.7 %all-to-all-done = bf16[8,2,16384]{2,1,0:T(2,128)(2,1)S(1)} async-done(((bf16[8,2,16384]{2,1,0:T(2,128)(2,1)}), bf16[8,2,16384]{2,1,0:T(2,128)(2,1)S(1)}, u32[]{:S(2)}, u32[]{:S(2)}) %all-to-all-start) | async-done | bytes 524320 | tf_op jit(solution)/shard_map/all_to_all | solution.py:57
  51.4 3.6 %all-to-all-start.4 = ((bf16[128,8,256]{2,0,1:T(8,128)(2,1)}), bf16[128,8,256]{2,0,1:T(8,128)(2,1)S(1)}, u32[]{:S(2)}, u32[]{:S(2)}) async-start(bf16[128,8,256]{2,0,1:T(8,128)(2,1)} %copy.68), calls=%async_computation.4 | async-start | bytes 1048576 | tf_op jit(solution)/shard_map/all_to_all | solution.py:62
  55.1 3.2 %copy.61 = bf16[128,8192]{0,1:T(8,128)(2,1)S(1)} copy(bf16[128,8192]{1,0:T(8,128)(2,1)} %param.8) | data formatting | bytes 4194304 | tf_op args[1]
  58.3 2.6 copy.62
  60.9 8.4 %all-to-all-done.4 = bf16[128,8,256]{2,0,1:T(8,128)(2,1)S(1)} async-done(((bf16[128,8,256]{2,0,1:T(8,128)(2,1)}), bf16[128,8,256]{2,0,1:T(8,128)(2,1)S(1)}, u32[]{:S(2)}, u32[]{:S(2)}) %all-to-all-start.4) | async-done | bytes 524320 | tf_op jit(solution)/shard_map/all_to_all | solution.py:62
  69.3 3.6 %all-to-all-start.1 = ((bf16[128,8,1024]{2,0,1:T(8,128)(2,1)}), bf16[128,8,1024]{2,0,1:T(8,128)(2,1)S(1)}, u32[]{:S(2)}, u32[]{:S(2)}) async-start(bf16[128,8,1024]{2,0,1:T(8,128)(2,1)} %copy.62), calls=%async_computation.1 | async-start | bytes 4194304 | tf_op jit(solution)/shard_map/all_to_all | solution.py:63
  75.1 2.2 copy.81
  77.9 4.1 %reshape.146 = bf16[8192,2,16]{2,1,0:T(2,128)(2,1)} reshape(bf16[8,2,16384]{2,1,0:T(2,128)(2,1)S(1)} %all-to-all-done) | data formatting | bytes 1048576
  82.0 8.9 %copy.79 = bf16[2,8,1024,16]{2,3,0,1:T(8,128)(2,1)S(1)} copy(bf16[2,8,1024,16]{3,0,2,1:T(2,128)(2,1)} %bitcast.71) | data formatting | bytes 1048576 | tf_op jit(solution)/shard_map/all_to_all | solution.py:57
  92.4 28.7 %all-to-all-done.1 = bf16[128,8,1024]{2,0,1:T(8,128)(2,1)S(1)} async-done(((bf16[128,8,1024]{2,0,1:T(8,128)(2,1)}), bf16[128,8,1024]{2,0,1:T(8,128)(2,1)S(1)}, u32[]{:S(2)}, u32[]{:S(2)}) %all-to-all-start.1) | async-done | bytes 2097184 | tf_op jit(solution)/shard_map/all_to_all | solution.py:63
  122.5 86.2 %all-reduce.3.cloned.1.call-done = (f32[8,128,16]{1,2,0:T(8,128)}, f32[8,128,16]{1,2,0:T(8,128)}) async-done(((f32[8,128,16]{1,2,0:T(8,128)}, f32[8,128,16]{1,2,0:T(8,128)}), (f32[8,128,16]{1,2,0:T(8,128)}, f32[8,128,16]{1,2,0:T(8,128)})) %all-reduce.3.cloned.1.call-update) | async-done | bytes 131088 | tf_op jit(solution)/shard_map/psum | solution.py:65
  217.0 6.4 %all-to-all-start.5 = ((bf16[16,256,16]{1,2,0:T(8,128)(2,1)}), bf16[16,256,16]{1,2,0:T(8,128)(2,1)S(1)}, u32[]{:S(2)}, u32[]{:S(2)}) async-start(bf16[16,256,16]{1,2,0:T(8,128)(2,1)} %copy.71), calls=%async_computation.5 | async-start | bytes 262144 | tf_op jit(solution)/shard_map/all_to_all | solution.py:92
  224.5 6.2 %all-to-all-done.5 = bf16[16,256,16]{1,2,0:T(8,128)(2,1)S(1)} async-done(((bf16[16,256,16]{1,2,0:T(8,128)(2,1)}), bf16[16,256,16]{1,2,0:T(8,128)(2,1)S(1)}, u32[]{:S(2)}, u32[]{:S(2)}) %all-to-all-start.5) | async-done | bytes 131104 | tf_op jit(solution)/shard_map/all_to_all | solution.py:92
  230.7 3.7 %all-to-all-start.3 = ((bf16[8,128,256]{2,1,0:T(8,128)(2,1)}), bf16[8,128,256]{2,1,0:T(8,128)(2,1)S(1)}, u32[]{:S(2)}, u32[]{:S(2)}) async-start(bf16[8,128,256]{2,1,0:T(8,128)(2,1)} %convolution_convert_fusion.1), calls=%async_computation.3 | async-start | bytes 1048576 | tf_op jit(solution)/shard_map/all_to_all | solution.py:91
  234.8 2.6 copy.73
  237.4 5.7 %reshape.125 = f32[8,16384]{1,0:T(8,128)S(1)} reshape(f32[8,1024,16]{2,1,0:T(8,128)} %copy.73) | data formatting | bytes 1048576 | tf_op jit(solution)/shard_map/reshape | solution.py:33
  243.1 3.4 %dot_general.47 = f32[1024,16,8]{1,0,2:T(8,128)} reshape(f32[16384,8]{0,1:T(8,128)S(1)} %bitcast.78) | data formatting | bytes 1048576 | tf_op jit(solution)/shard_map/dot_general | solution.py:34
  246.5 2.9 %copy.74 = f32[1024,16,8]{0,2,1:T(8,128)S(1)} copy(f32[1024,16,8]{1,0,2:T(8,128)} %dot_general.47) | data formatting | bytes 1048576 | tf_op jit(solution)/shard_map/dot_general | solution.py:34
  251.1 5.7 %all-to-all-start.6 = ((bf16[16,1024,16]{1,2,0:T(8,128)(2,1)}), bf16[16,1024,16]{1,2,0:T(8,128)(2,1)S(1)}, u32[]{:S(2)}, u32[]{:S(2)}) async-start(bf16[16,1024,16]{1,2,0:T(8,128)(2,1)} %copy.75), calls=%async_computation.6 | async-start | bytes 1048576 | tf_op jit(solution)/shard_map/all_to_all | solution.py:93
  258.8 8.8 %all-to-all-done.6 = bf16[16,1024,16]{1,2,0:T(8,128)(2,1)S(1)} async-done(((bf16[16,1024,16]{1,2,0:T(8,128)(2,1)}), bf16[16,1024,16]{1,2,0:T(8,128)(2,1)S(1)}, u32[]{:S(2)}, u32[]{:S(2)}) %all-to-all-start.6) | async-done | bytes 524320 | tf_op jit(solution)/shard_map/all_to_all | solution.py:93
  (48 shorter events, 24.9 us)
Async XLA Ops:
  7.2 11.1 %copy-start = (bf16[2,8192,16]{1,2,0:T(8,128)(2,1)S(1)}, bf16[2,8192,16]{1,2,0:T(8,128)(2,1)}, u32[]{:S(2)}) copy-start(bf16[2,8192,16]{1,2,0:T(8,128)(2,1)} %param.10) | copy-start | bytes 1572868
  11.0 20.5 %all-to-all-start.2 = ((bf16[8,2,4096]{2,1,0:T(2,128)(2,1)}), bf16[8,2,4096]{2,1,0:T(2,128)(2,1)S(1)}, u32[]{:S(2)}, u32[]{:S(2)}) async-start(bf16[8,2,4096]{2,1,0:T(2,128)(2,1)} %reshape.143), calls=%async_computation.2 | async-start | bytes 262144 | tf_op jit(solution)/shard_map/all_to_all | solution.py:56
  25.0 12.5 %copy-start.1 = (bf16[128,2048]{1,0:T(8,128)(2,1)S(1)}, bf16[128,2048]{1,0:T(8,128)(2,1)}, u32[]{:S(2)}) copy-start(bf16[128,2048]{1,0:T(8,128)(2,1)} %param.7) | copy-start | bytes 1572868
  31.5 19.9 %all-to-all-start = ((bf16[8,2,16384]{2,1,0:T(2,128)(2,1)}), bf16[8,2,16384]{2,1,0:T(2,128)(2,1)S(1)}, u32[]{:S(2)}, u32[]{:S(2)}) async-start(bf16[8,2,16384]{2,1,0:T(2,128)(2,1)} %reshape.145), calls=%async_computation | async-start | bytes 1048576 | tf_op jit(solution)/shard_map/all_to_all | solution.py:57
  51.4 17.9 %all-to-all-start.4 = ((bf16[128,8,256]{2,0,1:T(8,128)(2,1)}), bf16[128,8,256]{2,0,1:T(8,128)(2,1)S(1)}, u32[]{:S(2)}, u32[]{:S(2)}) async-start(bf16[128,8,256]{2,0,1:T(8,128)(2,1)} %copy.68), calls=%async_computation.4 | async-start | bytes 1048576 | tf_op jit(solution)/shard_map/all_to_all | solution.py:62
  60.9 12.0 %copy-start.4 = (s32[16]{0:T(128)S(1)}, s32[16]{0:T(128)}, u32[]{:S(2)}) copy-start(s32[16]{0:T(128)} %param.13) | copy-start | bytes 196
  60.9 12.0 %copy-start.5 = (s32[16]{0:T(128)S(1)}, s32[16]{0:T(128)}, u32[]{:S(2)}) copy-start(s32[16]{0:T(128)} %param.11) | copy-start | bytes 196
  60.9 12.1 %copy-start.6 = (s32[8]{0:T(128)S(1)}, s32[8]{0:T(128)}, u32[]{:S(2)}) copy-start(s32[8]{0:T(128)} %param.12) | copy-start | bytes 100
  69.3 51.8 %all-to-all-start.1 = ((bf16[128,8,1024]{2,0,1:T(8,128)(2,1)}), bf16[128,8,1024]{2,0,1:T(8,128)(2,1)S(1)}, u32[]{:S(2)}, u32[]{:S(2)}) async-start(bf16[128,8,1024]{2,0,1:T(8,128)(2,1)} %copy.62), calls=%async_computation.1 | async-start | bytes 4194304 | tf_op jit(solution)/shard_map/all_to_all | solution.py:63
  72.9 135.8 %all-reduce.3.cloned.1.call-start = ((), (), s32[]{:S(2)}) async-start(), calls=%async_computation.7 | async-start | bytes 262144 | tf_op jit(solution)/shard_map/psum | solution.py:65
  211.1 12.2 %copy-start.2 = (f32[8,128,16]{1,2,0:T(8,128)S(1)}, f32[8,128,16]{1,2,0:T(8,128)}, u32[]{:S(2)}) copy-start(f32[8,128,16]{1,2,0:T(8,128)} %get-tuple-element.17) | copy-start | bytes 196612
  214.3 20.0 %copy-start.3 = (f32[8,128,16]{1,2,0:T(8,128)S(1)}, f32[8,128,16]{1,2,0:T(8,128)}, u32[]{:S(2)}) copy-start(f32[8,128,16]{1,2,0:T(8,128)} %get-tuple-element.18) | copy-start | bytes 196612
  217.0 13.7 %all-to-all-start.5 = ((bf16[16,256,16]{1,2,0:T(8,128)(2,1)}), bf16[16,256,16]{1,2,0:T(8,128)(2,1)S(1)}, u32[]{:S(2)}, u32[]{:S(2)}) async-start(bf16[16,256,16]{1,2,0:T(8,128)(2,1)} %copy.71), calls=%async_computation.5 | async-start | bytes 262144 | tf_op jit(solution)/shard_map/all_to_all | solution.py:92
  230.7 20.4 %all-to-all-start.3 = ((bf16[8,128,256]{2,1,0:T(8,128)(2,1)}), bf16[8,128,256]{2,1,0:T(8,128)(2,1)S(1)}, u32[]{:S(2)}, u32[]{:S(2)}) async-start(bf16[8,128,256]{2,1,0:T(8,128)(2,1)} %convolution_convert_fusion.1), calls=%async_computation.3 | async-start | bytes 1048576 | tf_op jit(solution)/shard_map/all_to_all | solution.py:91
  251.1 16.5 %all-to-all-start.6 = ((bf16[16,1024,16]{1,2,0:T(8,128)(2,1)}), bf16[16,1024,16]{1,2,0:T(8,128)(2,1)S(1)}, u32[]{:S(2)}, u32[]{:S(2)}) async-start(bf16[16,1024,16]{1,2,0:T(8,128)(2,1)} %copy.75), calls=%async_computation.6 | async-start | bytes 1048576 | tf_op jit(solution)/shard_map/all_to_all | solution.py:93
Sparse Core Ops, SparseCore 0:
  122.6 86.1 all-reduce.2
where the time goes:
time: 277 us; the launch traced here: 275 us
  waiting for transfers between devices  151 us (55%)
  local copies, waits for them, and re-layouts  67.6 us (24%)
  starting transfers between devices  36.3 us (13%)
  between operations  14.2 us (5%)
  matrix products  5.78 us (2%)
    psum x1, waiting for transfers between devices, on_device(): lax.psum((rank_terms(input_cols, down_factor_blocks, nblocks), rank_terms...  86.2 us
    all_to_all x1, waiting for transfers between devices, on_device(): lax.all_to_all(cotangent, 'rows', split_axis=1, concat_axis=0, tiled=True)  28.7 us
    unnamed x23, local copies, waits for them, and re-layouts  27.4 us
    all_to_all x1, waiting for transfers between devices, on_device(): lax.all_to_all(adapter_up_factors, 'rows', split_axis=1, concat_axis=0, t...  12.7 us
    dot_general x4, local copies, waits for them, and re-layouts, slot_total(): jnp.dot(selector, flat, precision=lax.Precision.HIGHEST, preferred_elemen...  9.17 us
    all_to_all x1, local copies, waits for them, and re-layouts, on_device(): lax.all_to_all(adapter_up_factors, 'rows', split_axis=1, concat_axis=0, t...  8.9 us
    all_to_all x1, waiting for transfers between devices, on_device(): lax.all_to_all(grad_up_cols, 'rows', split_axis=0, concat_axis=1, tiled=T...  8.79 us
    all_to_all x1, waiting for transfers between devices, on_device(): lax.all_to_all(activations, 'rows', split_axis=1, concat_axis=0, tiled=True)  8.35 us
  transfers between devices with their start and end apart: 8, of which 6 were waited for; matrix products, arithmetic and copies ran while one was open for 22% of the time, Pallas kernels for 0%

commit v1 on v0

--- a/solution.py
+++ b/solution.py
@@ -95,6 +95,74 @@
     return (input_grad, grad_down, grad_up)
 
 
+GATHER_LIMIT = 24 << 20
+
+
+def tenant_plan(
+    activations,
+    cotangent,
+    adapter_down_factors,
+    adapter_up_factors,
+    adapter_slot,
+    adapter_of_block,
+    counts,
+):
+    active_rows, slot_of_block = row_plan(adapter_of_block, counts, adapter_slot)
+    me = lax.axis_index("rows")
+    inputs = activations.shape[1]
+    mine = jnp.concatenate(
+        [jnp.swapaxes(adapter_down_factors, 1, 2), jnp.swapaxes(adapter_up_factors, 1, 2)], axis=2
+    )
+    factors = lax.all_gather(mine, "rows", axis=0, tiled=True)
+    factor = lax.dynamic_index_in_dim(factors, slot_of_block[me], 0, keepdims=False)
+    live = lax.dynamic_index_in_dim(active_rows, me, 0, keepdims=False)[:, None]
+    sums = jnp.concatenate(
+        [
+            lax.dot_general(activations, factor[:, :inputs], (((1,), (1,)), ((), ())),
+                            preferred_element_type=jnp.float32),
+            lax.dot_general(cotangent, factor[:, inputs:], (((1,), (1,)), ((), ())),
+                            preferred_element_type=jnp.float32),
+        ],
+        axis=1,
+    )
+    sums = lax.psum(sums, "tp")
+    rank = factor.shape[0]
+    low_down = (live * sums[:, :rank]).astype(jnp.bfloat16)
+    low_up = (adapter_scale * live * sums[:, rank:]).astype(jnp.bfloat16)
+    input_grad = jnp.dot(low_up, factor[:, :inputs], preferred_element_type=jnp.float32)
+    over_rows = (((0,), (0,)), ((), ()))
+    terms = jnp.concatenate(
+        [
+            lax.dot_general(low_up, activations, over_rows, preferred_element_type=jnp.float32),
+            adapter_scale
+            * lax.dot_general(low_down, cotangent, over_rows, preferred_element_type=jnp.float32),
+        ],
+        axis=1,
+    ).astype(jnp.bfloat16)
+    every = lax.all_gather(terms, "rows", axis=0, tiled=False).astype(jnp.float32)
+    here = adapter_down_factors.shape[0]
+    grads = jnp.stack(
+        [
+            jnp.sum(
+                jnp.where((slot_of_block == me * here + at)[:, None, None], every, 0.0), axis=0
+            )
+            for at in range(here)
+        ]
+    ).astype(jnp.bfloat16)
+    return (
+        input_grad.astype(jnp.bfloat16),
+        jnp.swapaxes(grads[:, :, :inputs], 1, 2),
+        jnp.swapaxes(grads[:, :, inputs:], 1, 2),
+    )
+
+
+def choose(*args):
+    factors = (args[2].size + args[3].size) * 2 * jax.lax.axis_size("rows")
+    one_block = args[0].shape[0] == BLK
+    plan = tenant_plan if one_block and factors <= GATHER_LIMIT else on_device
+    return plan(*args)
+
+
 def solution(mesh):
     in_specs = (
         P(("groups", "rows"), "tp"),
@@ -111,5 +179,5 @@
         P(("groups", "rows"), "tp", None),
     )
     return jax.shard_map(
-        on_device, mesh=mesh, in_specs=in_specs, out_specs=out_specs, check_vma=False
+        choose, mesh=mesh, in_specs=in_specs, out_specs=out_specs, check_vma=False
     )

time: 277 us -> 170 us (0.61)
  local copies, waits for them, and re-layouts: 67.6 us -> 1.6 us
  starting transfers between devices: 36.3 us -> 0.08 us
  waiting for transfers between devices: 151 us -> 137 us
  other arithmetic: 0.46 us -> 9.03 us
  blocking collectives: 0 us -> 3.37 us
  matrix products: 5.78 us -> 2.58 us
    all_gather x0 -> x2, waiting for transfers between devices: none -> 137 us  [the longest x1 85.3 us: tenant_plan(): factors = lax.all_gather(mine, 'rows', axis=0, tiled=True)]
    psum x1 -> x0, waiting for transfers between devices: 86.2 us -> none  [on_device(): lax.psum((rank_terms(input_cols, down_factor_blocks, nblocks), rank_terms...]
    all_to_all x7 -> x0, waiting for transfers between devices: 64.7 us -> none  [the longest x1 28.7 us: on_device(): lax.all_to_all(cotangent, 'rows', split_axis=1, concat_axis=0, tiled=True)]
    all_to_all x7 -> x0, starting transfers between devices: 36.3 us -> none  [the longest x1 7.25 us: on_device(): lax.all_to_all(adapter_down_factors, 'rows', split_axis=1, concat_axis=0,...]
    unnamed x23 -> x4, local copies, waits for them, and re-layouts: 27.4 us -> 0.01 us
    all_to_all x7 -> x0, local copies, waits for them, and re-layouts: 16.6 us -> none  [the longest x1 8.9 us: on_device(): lax.all_to_all(adapter_up_factors, 'rows', split_axis=1, concat_axis=0, t...]
    dot_general x5 -> x0, local copies, waits for them, and re-layouts: 10.5 us -> none  [the longest x4 9.17 us: slot_total(): jnp.dot(selector, flat, precision=lax.Precision.HIGHEST, preferred_elemen...]
    reshape x2 -> x0, local copies, waits for them, and re-layouts: 7.56 us -> none  [slot_total(): flat = terms.reshape(terms.shape[0], -1)]
  transfers between devices with their start and end apart: 8 -> 2, of which waited for: 6 -> 2; matrix products, arithmetic and copies ran while one was open for 22% -> 2% of each run, Pallas kernels for 0% -> 0%
where the time goes in v1:
time: 170 us
  waiting for transfers between devices  137 us (81%)
  between operations  16 us (9%)
  other arithmetic  9.03 us (5%)
  blocking collectives  3.37 us (2%)
  matrix products  2.58 us (2%)
    all_gather x1, waiting for transfers between devices, tenant_plan(): factors = lax.all_gather(mine, 'rows', axis=0, tiled=True)  85.3 us
    all_gather x1, waiting for transfers between devices, tenant_plan(): lax.all_gather(terms, 'rows', axis=0, tiled=False).astype(jnp.float32)  51.9 us
  transfers between devices with their start and end apart: 2, of which 2 were waited for; matrix products, arithmetic and copies ran while one was open for 2% of the time, Pallas kernels for 0%

profile of v1, /device:TPU:0, one launch (start us, length us, event | category | flops | bytes accessed | tf_op | source)
XLA Modules:
  0.0 169.9 jit_solution(6648713557668980199)
XLA Ops:
  7.2 0.0 copy-start
  7.2 0.0 all-gather.3.cloned.1.call-start
  7.2 2.1 %pad_maximum_fusion = bf16[2,16,10240]{2,1,0:T(8,128)(2,1)} fusion(bf16[2,16,8192]{2,1,0:T(8,128)(2,1)} %bitcast.34, bf16[2,16,2048]{2,1,0:T(8,128)(2,1)} %bitcast.35), kind=kLoop, calls=%fused_computation.12 | loop fusion | flops 1310720 | bytes 1310720 | tf_op jit(solution)/shard_map/concatenate | solution.py:113
  9.3 0.0 all-gather.3.cloned.1.call-update
  9.4 0.0 all-gather.5.cloned.1.call-start
  9.4 0.9 select_reduce_fusion.1
  10.3 0.6 dynamic_slice.12
  12.9 0.9 select_reduce_fusion.2
  13.8 0.1 fusion.14
  13.9 85.3 %all-gather.3.cloned.1.call-done = bf16[16,16,10240]{2,1,0:T(8,128)(2,1)} async-done(((bf16[2,16,10240]{2,1,0:T(8,128)(2,1)}), bf16[16,16,10240]{2,1,0:T(8,128)(2,1)}) %all-gather.3.cloned.1.call-update) | async-done | bytes 5242896 | tf_op jit(solution)/shard_map/all_gather | solution.py:116
  99.2 1.0 dynamic-slice_bitcast_fusion
  100.2 0.0 copy-done
  100.2 0.6 convolution_bitcast_fusion
  100.8 0.3 convolution_bitcast_fusion.1
  101.1 3.4 %psum.7 = f32[128,32]{0,1:T(8,128)S(1)} all-reduce(f32[128,32]{0,1:T(8,128)S(1)} %pad_maximum_fusion.3), channel_id=1, replica_groups=mesh['groups'=2,'rows'=8,'tp'=2] {'tp'}, use_global_device_ids=true, to_apply=%region_3.4 | all-reduce | flops 4096 | bytes 32768 | tf_op jit(solution)/shard_map/psum | solution.py:128
  104.5 0.4 fusion.1
  104.9 0.2 fusion.4
  105.0 0.8 pad_maximum_fusion.2
  105.8 0.0 all-gather.5.cloned.1.call-update
  105.8 1.1 convolution_convert_fusion
  107.0 51.9 %all-gather.5.cloned.1.call-done = bf16[8,16,10240]{2,1,0:T(8,128)(2,1)} async-done(((bf16[1,16,10240]{2,1,0:T(8,128)(2,1)}), bf16[8,16,10240]{2,1,0:T(8,128)(2,1)}) %all-gather.5.cloned.1.call-update) | async-done | bytes 2621456 | tf_op jit(solution)/shard_map/all_gather | solution.py:142
  158.8 2.7 %fusion.2 = (bf16[16,10240]{1,0:T(8,128)(2,1)S(1)}, bf16[16,10240]{1,0:T(8,128)(2,1)S(1)}) fusion(bf16[8,16,10240]{2,1,0:T(8,128)(2,1)} %all-gather.5.cloned.1.call-done, pred[8]{0:T(512)(128)(4,1)S(1)} %get-tuple-element.10, pred[8]{0:T(512)(128)(4,1)S(1)} %get-tuple-element.9), kind=kLoop, calls=%fused_computation.5 | loop fusion | flops 6225920 | bytes 3276816 | tf_op jit(solution)/shard_map/reduce_sum | solution.py:146
  161.6 0.7 maximum_bitcast_fusion
  162.2 0.8 fusion.5
  (6 shorter events, 0.0 us)
Async XLA Ops:
  7.2 93.0 %copy-start = (bf16[128,8192]{1,0:T(8,128)(2,1)S(1)}, bf16[128,8192]{1,0:T(8,128)(2,1)}, u32[]{:S(2)}) copy-start(bf16[128,8192]{1,0:T(8,128)(2,1)} %param.8) | copy-start | bytes 6291460
  7.2 92.0 %all-gather.3.cloned.1.call-start = ((), (), s32[]{:S(2)}) async-start(), calls=%async_computation | async-start | bytes 5898240 | tf_op jit(solution)/shard_map/all_gather | solution.py:116
  9.3 91.5 %copy-start.1 = (bf16[128,2048]{1,0:T(8,128)(2,1)S(1)}, bf16[128,2048]{1,0:T(8,128)(2,1)}, u32[]{:S(2)}) copy-start(bf16[128,2048]{1,0:T(8,128)(2,1)} %param.7) | copy-start | bytes 1572868
  9.4 149.5 %all-gather.5.cloned.1.call-start = ((), (), s32[]{:S(2)}) async-start(), calls=%async_computation.1 | async-start | bytes 2949120 | tf_op jit(solution)/shard_map/all_gather | solution.py:142
Sparse Core Ops, SparseCore 0:
  10.2 88.9 all-gather.2
  105.9 52.8 all-gather.4

commit v2 on v0

--- a/solution.py
+++ b/solution.py
@@ -1,6 +1,10 @@
+import functools
+
 import jax
 import jax.numpy as jnp
 from jax import lax
+from jax.experimental import pallas as pl
+from jax.experimental.pallas import tpu as pltpu
 from jax.sharding import PartitionSpec as P
 
 BLK = 128
@@ -95,6 +99,307 @@
     return (input_grad, grad_down, grad_up)
 
 
+GATHER_LIMIT = 24 << 20
+
+
+LANES = 2
+MESH = pl.DeviceIdType.MESH
+NT = (((1,), (1,)), ((), ()))
+TN = (((0,), (0,)), ((), ()))
+
+
+def line_gather(buf, piece, send, recv, rows):
+    line = rows // LANES
+    me = lax.axis_index("rows")
+    at, lane = me // LANES, me % LANES
+
+    def copy(where, p, to):
+        return pltpu.make_async_remote_copy(
+            src_ref=piece(buf, p),
+            dst_ref=piece(buf, p),
+            send_sem=send.at[where, p // LANES],
+            recv_sem=recv.at[p],
+            device_id={"rows": to},
+            device_id_type=MESH,
+        )
+
+    def arrived(p):
+        copy(0, p, me ^ 1).wait_recv()
+
+    def start():
+        @pl.when(at < line - 1)
+        def _():
+            copy(0, me, me + LANES).start()
+
+        @pl.when(at > 0)
+        def _():
+            copy(1, me, me - LANES).start()
+
+        copy(2, me, me ^ 1).start()
+
+    def forward():
+        for k in range(1, line):
+            low, high = me - k * LANES, me + k * LANES
+
+            @pl.when(at - k >= 0)
+            def _():
+                arrived(low)
+
+                @pl.when(at < line - 1)
+                def _():
+                    copy(0, low, me + LANES).start()
+
+                copy(2, low, me ^ 1).start()
+
+            @pl.when(at + k < line)
+            def _():
+                arrived(high)
+
+                @pl.when(at > 0)
+                def _():
+                    copy(1, high, me - LANES).start()
+
+                copy(2, high, me ^ 1).start()
+
+        for z in range(line):
+            arrived(z * LANES + 1 - lane)
+
+    def drain():
+        for z in range(line):
+            p = z * LANES + lane
+            copy(2, p, me ^ 1).wait_send()
+
+            @pl.when(jnp.logical_and(z <= at, at < line - 1))
+            def _():
+                copy(0, p, me + LANES).wait_send()
+
+            @pl.when(jnp.logical_and(z >= at, at > 0))
+            def _():
+                copy(1, p, me - LANES).wait_send()
+
+    return start, forward, drain
+
+
+def tenant_kernel(
+    rows,
+    wanted,
+    block_slots,
+    live,
+    mine,
+    act_hbm,
+    cot_hbm,
+    input_grad,
+    grad_down,
+    grad_up,
+    fac,
+    terms,
+    act,
+    cot,
+    half_out,
+    half_in,
+    sum_out,
+    sum_in,
+    fac_send,
+    fac_recv,
+    term_send,
+    term_recv,
+    pair_send,
+    pair_recv,
+    local,
+):
+    me = lax.axis_index("rows")
+    group = lax.axis_index("groups")
+    core = lax.axis_index("tp")
+    line = rows // LANES
+    at = me // LANES
+    here = mine.shape[0]
+    inputs = act.shape[1]
+    hidden = cot.shape[1]
+    ih, hh = inputs // 2, hidden // 2
+
+    loads = [
+        pltpu.make_async_copy(act_hbm, act, local.at[0]),
+        pltpu.make_async_copy(cot_hbm, cot, local.at[1]),
+    ]
+    for load in loads:
+        load.start()
+    fac[pl.ds(me * here, here)] = mine[...]
+
+    barrier = pltpu.get_barrier_semaphore()
+
+    def greet(target):
+        pl.semaphore_signal(barrier, inc=1, device_id=target, device_id_type=MESH)
+
+    greet({"rows": me ^ 1})
+    greet({"groups": 1 - group})
+    greet({"tp": 1 - core})
+
+    @pl.when(at > 0)
+    def _():
+        greet({"rows": me - LANES})
+
+    @pl.when(at < line - 1)
+    def _():
+        greet({"rows": me + LANES})
+
+    pl.semaphore_wait(
+        barrier, 3 + jnp.where(at > 0, 1, 0) + jnp.where(at < line - 1, 1, 0)
+    )
+
+    start, forward, drain = line_gather(
+        fac, lambda r, p: r.at[pl.ds(p * here, here)], fac_send, fac_recv, rows
+    )
+    start()
+    forward()
+
+    half_out[...] = fac[wanted[1]]
+    swap = pltpu.make_async_remote_copy(
+        src_ref=half_out,
+        dst_ref=half_in,
+        send_sem=pair_send.at[0],
+        recv_sem=pair_recv.at[0],
+        device_id={"groups": 1 - group},
+        device_id_type=MESH,
+    )
+    swap.start()
+    own = fac[wanted[0]]
+    for load in loads:
+        load.wait()
+    swap.wait_recv()
+    other = half_in[...]
+    first = group == 0
+    left = jnp.where(first, own, other)
+    right = jnp.where(first, other, own)
+
+    def dot(a, b, dims=(((1,), (0,)), ((), ()))):
+        return lax.dot_general(a, b, dims, preferred_element_type=jnp.float32)
+
+    rank = left.shape[0]
+    sum_out[0:rank] = dot(left[:, :ih], act[:, :ih], NT) + dot(right[:, :ih], act[:, ih:], NT)
+    sum_out[rank:] = dot(left[:, ih:], cot[:, :hh], NT) + dot(right[:, ih:], cot[:, hh:], NT)
+    pair = pltpu.make_async_remote_copy(
+        src_ref=sum_out,
+        dst_ref=sum_in,
+        send_sem=pair_send.at[1],
+        recv_sem=pair_recv.at[1],
+        device_id={"tp": 1 - core},
+        device_id_type=MESH,
+    )
+    pair.start()
+    pair.wait_recv()
+    sums = sum_out[...] + sum_in[...]
+    low_down = (live[...] * sums[:rank]).astype(jnp.bfloat16)
+    low_up = (adapter_scale * live[...] * sums[rank:]).astype(jnp.bfloat16)
+
+    terms[me, :, 0:inputs] = dot(low_up, act[...]).astype(jnp.bfloat16)
+    terms[me, :, inputs:] = (adapter_scale * dot(low_down, cot[...])).astype(jnp.bfloat16)
+    start2, forward2, drain2 = line_gather(
+        terms, lambda r, p: r.at[p], term_send, term_recv, rows
+    )
+    start2()
+    input_grad[:, 0:ih] = dot(low_up, left[:, :ih], TN).astype(jnp.bfloat16)
+    input_grad[:, ih:] = dot(low_up, right[:, :ih], TN).astype(jnp.bfloat16)
+    forward2()
+
+    tile = 512
+    for out, base, width in ((grad_down, 0, inputs), (grad_up, inputs, hidden)):
+
+        def add(i, carry, out=out, base=base):
+            to = pl.ds(pl.multiple_of(i * tile, tile), tile)
+            source = pl.ds(pl.multiple_of(base + i * tile, tile), tile)
+            totals = [jnp.zeros((rank, tile), jnp.float32) for _ in range(here)]
+            for b in range(rows):
+                term = terms[b, :, source].astype(jnp.float32)
+                for j in range(here):
+                    mask = jnp.where(block_slots[b] == me * here + j, 1.0, 0.0)
+                    totals[j] += mask * term
+            for j in range(here):
+                out[j, :, to] = totals[j].astype(jnp.bfloat16)
+            return carry
+
+        lax.fori_loop(0, width // tile, add, 0)
+
+    drain()
+    drain2()
+    swap.wait_send()
+    pair.wait_send()
+
+
+def tenant_plan(
+    activations,
+    cotangent,
+    adapter_down_factors,
+    adapter_up_factors,
+    adapter_slot,
+    adapter_of_block,
+    counts,
+):
+    active_rows, slot_of_block = row_plan(adapter_of_block, counts, adapter_slot)
+    rows = jax.lax.axis_size("rows")
+    me = lax.axis_index("rows")
+    group = lax.axis_index("groups")
+    here, inputs, rank = adapter_down_factors.shape
+    hidden = adapter_up_factors.shape[1]
+    half = (inputs + hidden) // 2
+    down = jnp.swapaxes(adapter_down_factors, 1, 2)
+    up = jnp.swapaxes(adapter_up_factors, 1, 2)
+    mine = jnp.concatenate(
+        [
+            lax.dynamic_slice_in_dim(down, group * (inputs // 2), inputs // 2, 2),
+            lax.dynamic_slice_in_dim(up, group * (hidden // 2), hidden // 2, 2),
+        ],
+        axis=2,
+    )
+    slot = slot_of_block[me]
+    both = lax.all_gather(slot_of_block, "groups")
+    wanted = jnp.stack([slot, both[1 - group, me]])
+    live = lax.dynamic_slice_in_dim(active_rows, me, 1, 0)
+    bf16, f32 = jnp.bfloat16, jnp.float32
+    line = rows // LANES
+    vmem = pl.BlockSpec(memory_space=pltpu.VMEM)
+    smem = pl.BlockSpec(memory_space=pltpu.SMEM)
+    hbm = pl.BlockSpec(memory_space=pl.ANY)
+    dma = pltpu.SemaphoreType.DMA
+    input_grad, grad_down, grad_up = pl.pallas_call(
+        functools.partial(tenant_kernel, rows),
+        out_shape=(
+            jax.ShapeDtypeStruct((BLK, inputs), bf16),
+            jax.ShapeDtypeStruct((here, rank, inputs), bf16),
+            jax.ShapeDtypeStruct((here, rank, hidden), bf16),
+        ),
+        in_specs=[smem, smem, vmem, vmem, hbm, hbm],
+        out_specs=(vmem, vmem, vmem),
+        scratch_shapes=[
+            pltpu.VMEM((rows * here, rank, half), bf16),
+            pltpu.VMEM((rows, rank, inputs + hidden), bf16),
+            pltpu.VMEM((BLK, inputs), bf16),
+            pltpu.VMEM((BLK, hidden), bf16),
+            pltpu.VMEM((rank, half), bf16),
+            pltpu.VMEM((rank, half), bf16),
+            pltpu.VMEM((2 * rank, BLK), f32),
+            pltpu.VMEM((2 * rank, BLK), f32),
+            dma((3, line)),
+            dma((rows,)),
+            dma((3, line)),
+            dma((rows,)),
+            dma((2,)),
+            dma((2,)),
+            dma((2,)),
+        ],
+        compiler_params=pltpu.CompilerParams(
+            collective_id=0, has_side_effects=True, vmem_limit_bytes=40 << 20
+        ),
+    )(wanted, slot_of_block, live, mine, activations, cotangent)
+    return input_grad, jnp.swapaxes(grad_down, 1, 2), jnp.swapaxes(grad_up, 1, 2)
+
+
+def choose(*args):
+    factors = (args[2].size + args[3].size) * 2 * jax.lax.axis_size("rows")
+    one_block = args[0].shape[0] == BLK
+    plan = tenant_plan if one_block and jax.lax.axis_size("groups") == 2 and factors <= GATHER_LIMIT else on_device
+    return plan(*args)
+
+
 def solution(mesh):
     in_specs = (
         P(("groups", "rows"), "tp"),
@@ -111,5 +416,5 @@
         P(("groups", "rows"), "tp", None),
     )
     return jax.shard_map(
-        on_device, mesh=mesh, in_specs=in_specs, out_specs=out_specs, check_vma=False
-    )
+        choose, mesh=mesh, in_specs=in_specs, out_specs=out_specs, check_vma=False
+    )

time: 277 us -> 95.5 us (0.34)
  waiting for transfers between devices: 151 us -> 0 us
  Pallas kernels: 0 us -> 76.8 us
  local copies, waits for them, and re-layouts: 67.6 us -> 8.5 us
  starting transfers between devices: 36.3 us -> 0 us
  between operations: 14.2 us -> 1.34 us
  matrix products: 5.78 us -> 0 us
  blocking collectives: 0 us -> 5.22 us
  other arithmetic: 0.46 us -> 3.28 us
    psum x1 -> x0, waiting for transfers between devices: 86.2 us -> none  [on_device(): lax.psum((rank_terms(input_cols, down_factor_blocks, nblocks), rank_terms...]
    pallas_call x0 -> x1, Pallas kernels: none -> 76.8 us  [tenant_plan(): pl.pallas_call(functools.partial(tenant_kernel, rows), out_shape=(jax.Sha...]
    all_to_all x7 -> x0, waiting for transfers between devices: 64.7 us -> none  [the longest x1 28.7 us: on_device(): lax.all_to_all(cotangent, 'rows', split_axis=1, concat_axis=0, tiled=True)]
    all_to_all x7 -> x0, starting transfers between devices: 36.3 us -> none  [the longest x1 7.25 us: on_device(): lax.all_to_all(adapter_down_factors, 'rows', split_axis=1, concat_axis=0,...]
    unnamed x23 -> x12, local copies, waits for them, and re-layouts: 27.4 us -> 6.37 us
    all_to_all x7 -> x0, local copies, waits for them, and re-layouts: 16.6 us -> none  [the longest x1 8.9 us: on_device(): lax.all_to_all(adapter_up_factors, 'rows', split_axis=1, concat_axis=0, t...]
    dot_general x5 -> x0, local copies, waits for them, and re-layouts: 10.5 us -> none  [the longest x4 9.17 us: slot_total(): jnp.dot(selector, flat, precision=lax.Precision.HIGHEST, preferred_elemen...]
    reshape x2 -> x0, local copies, waits for them, and re-layouts: 7.56 us -> none  [slot_total(): flat = terms.reshape(terms.shape[0], -1)]
  transfers between devices with their start and end apart: 8 -> 0, of which waited for: 6 -> 0; matrix products, arithmetic and copies ran while one was open for 22% -> 0% of each run, Pallas kernels for 0% -> 0%
where the time goes in v2:
time: 95.5 us; the launch traced here: 95.1 us
  Pallas kernels  76.8 us (80%)
  local copies, waits for them, and re-layouts  8.5 us (9%)
  blocking collectives  5.22 us (5%)
  other arithmetic  3.28 us (3%)
  between operations  1.34 us (1%)
    pallas_call x1, Pallas kernels, tenant_plan(): pl.pallas_call(functools.partial(tenant_kernel, rows), out_shape=(jax.Sha...  76.8 us
    unnamed x12, local copies, waits for them, and re-layouts  6.37 us
    unnamed x1, blocking collectives  5.22 us

profile of v2, /device:TPU:0, one launch (start us, length us, event | category | flops | bytes accessed | tf_op | source)
XLA Modules:
  0.0 95.1 jit_solution(17432378455704007056)
XLA Ops:
  0.6 0.0 copy-start
  0.7 1.3 %dynamic-slice.8 = u32[1]{0:T(128)} dynamic-slice(u32[32]{0:T(128)} %constant.37, u32[]{:T(128)S(6)} %add.35), dynamic_slice_sizes={1} | dynamic-slice | bytes 12
  2.6 0.9 select_reduce_fusion.1
  3.5 0.9 select_reduce_fusion
  4.4 0.6 dynamic_slice.15
  5.0 0.2 dynamic-update-slice
  5.2 0.1 reshape.15
  5.3 5.2 %all-reduce.1 = s32[2,8]{1,0:T(2,128)S(1)} all-reduce(s32[2,8]{1,0:T(2,128)S(1)} %reshape.15), channel_id=2, replica_groups=mesh['groups'=2,'rows'=8,'tp'=2] {'groups'}, use_global_device_ids=true, to_apply=%add | all-reduce | flops 16 | bytes 128
  10.5 0.6 dynamic_slice.16
  11.1 1.4 %pad_add_fusion.wanted = s32[2]{0:T(128)S(1)} fusion(s32[1]{0:T(128)} %bitcast.1, s32[1]{0:T(128)} %dynamic_slice.15), kind=kLoop, calls=%fused_computation.12 | loop fusion | flops 2 | bytes 16 | tf_op jit(solution)/shard_map/stack | solution.py:355
  12.5 0.1 fusion.1
  12.5 0.8 dynamic-slice_bitcast_fusion.1
  13.4 0.0 copy-done
  13.4 0.0 copy-start.1
  13.5 1.6 %copy-done.1 = bf16[128,8192]{1,0:T(8,128)(2,1)S(1)} copy-done((bf16[128,8192]{1,0:T(8,128)(2,1)S(1)}, bf16[128,8192]{1,0:T(8,128)(2,1)}, u32[]{:S(2)}) %copy-start.1) | copy-done | bytes 2097176
  15.0 0.0 copy-start.2
  15.0 1.0 %copy-done.2 = bf16[128,2048]{1,0:T(8,128)(2,1)S(1)} copy-done((bf16[128,2048]{1,0:T(8,128)(2,1)S(1)}, bf16[128,2048]{1,0:T(8,128)(2,1)}, u32[]{:S(2)}) %copy-start.2) | copy-done | bytes 524312
  16.1 76.8 %shard_map.94 = (bf16[128,2048]{1,0:T(8,128)(2,1)S(1)}, bf16[2,16,2048]{2,1,0:T(8,128)(2,1)S(1)}, bf16[2,16,8192]{2,1,0:T(8,128)(2,1)S(1)}) custom-call(s32[2]{0:T(128)S(1)} %pad_add_fusion.wanted, s32[8]{0:T(128)S(1)} %get-tuple-element.10.block_slots, f32[1,128]{1,0:T(1,128)S(1)} %constant_dynamic-slice_fusion.live, ...), custom_call_target="tpu_custom_call" | custom-call | tf_op jit(solution)/shard_map/pallas_call | solution.py:363
  92.8 0.8 copy.14
  93.6 0.7 copy.15
  94.3 0.8 copy.16
  (5 shorter events, 0.1 us)
Async XLA Ops:
  0.6 12.8 %copy-start = (bf16[2,8192,16]{1,2,0:T(8,128)(2,1)S(1)}, bf16[2,8192,16]{1,2,0:T(8,128)(2,1)}, u32[]{:S(2)}) copy-start(bf16[2,8192,16]{1,2,0:T(8,128)(2,1)} %param.10) | copy-start | bytes 1572868
  13.4 1.6 %copy-start.1 = (bf16[128,8192]{1,0:T(8,128)(2,1)S(1)}, bf16[128,8192]{1,0:T(8,128)(2,1)}, u32[]{:S(2)}) copy-start(bf16[128,8192]{1,0:T(8,128)(2,1)} %cot_hbm.1) | copy-start | bytes 6291460
  15.0 1.0 %copy-start.2 = (bf16[128,2048]{1,0:T(8,128)(2,1)S(1)}, bf16[128,2048]{1,0:T(8,128)(2,1)}, u32[]{:S(2)}) copy-start(bf16[128,2048]{1,0:T(8,128)(2,1)} %act_hbm.1) | copy-start | bytes 1572868

commit v3 on v2

--- a/solution.py
+++ b/solution.py
@@ -161,6 +161,7 @@
 
                 copy(2, high, me ^ 1).start()
 
+    def beside():
         for z in range(line):
             arrived(z * LANES + 1 - lane)
 
@@ -177,15 +178,16 @@
             def _():
                 copy(1, p, me - LANES).wait_send()
 
-    return start, forward, drain
+    return start, forward, beside, drain
 
 
 def tenant_kernel(
     rows,
-    wanted,
-    block_slots,
-    live,
-    mine,
+    slot_of,
+    block_adapter,
+    counts,
+    down_hbm,
+    up_hbm,
     act_hbm,
     cot_hbm,
     input_grad,
@@ -193,12 +195,16 @@
     grad_up,
     fac,
     terms,
+    totals,
     act,
     cot,
     half_out,
     half_in,
     sum_out,
     sum_in,
+    wish_out,
+    wish_in,
+    wish,
     fac_send,
     fac_recv,
     term_send,
@@ -211,19 +217,32 @@
     group = lax.axis_index("groups")
     core = lax.axis_index("tp")
     line = rows // LANES
-    at = me // LANES
-    here = mine.shape[0]
-    inputs = act.shape[1]
+    at, lane = me // LANES, me % LANES
+    here, rank, inputs = grad_down.shape
     hidden = cot.shape[1]
     ih, hh = inputs // 2, hidden // 2
-
+    spot = pl.ds(me * here, here)
+
+    own_factors = [
+        pltpu.make_async_copy(
+            down_hbm.at[:, :, pl.ds(pl.multiple_of(group * ih, 128), ih)],
+            fac.at[spot, :, pl.ds(0, ih)],
+            local.at[2],
+        ),
+        pltpu.make_async_copy(
+            up_hbm.at[:, :, pl.ds(pl.multiple_of(group * hh, 128), hh)],
+            fac.at[spot, :, pl.ds(ih, hh)],
+            local.at[3],
+        ),
+    ]
+    for load in own_factors:
+        load.start()
     loads = [
         pltpu.make_async_copy(act_hbm, act, local.at[0]),
         pltpu.make_async_copy(cot_hbm, cot, local.at[1]),
     ]
     for load in loads:
         load.start()
-    fac[pl.ds(me * here, here)] = mine[...]
 
     barrier = pltpu.get_barrier_semaphore()
 
@@ -242,87 +261,122 @@
     def _():
         greet({"rows": me + LANES})
 
+    adapter = block_adapter[me]
+    slot = slot_of[adapter]
+    earlier = jnp.int32(0)
+    for b in range(rows):
+        same = jnp.logical_and(block_adapter[b] == adapter, b < me)
+        earlier += jnp.where(same, 1, 0)
+    place = lax.broadcasted_iota(jnp.int32, (1, BLK), 1)
+    live = jnp.where(earlier * BLK + place < counts[adapter], 1.0, 0.0)
+    wish_out[...] = jnp.full(wish_out.shape, slot, jnp.int32)
+
+    for load in own_factors:
+        load.wait()
     pl.semaphore_wait(
         barrier, 3 + jnp.where(at > 0, 1, 0) + jnp.where(at < line - 1, 1, 0)
     )
 
-    start, forward, drain = line_gather(
+    def pair(source, target, which, to):
+        return pltpu.make_async_remote_copy(
+            src_ref=source,
+            dst_ref=target,
+            send_sem=pair_send.at[which],
+            recv_sem=pair_recv.at[which],
+            device_id=to,
+            device_id_type=MESH,
+        )
+
+    start, forward, beside, drain = line_gather(
         fac, lambda r, p: r.at[pl.ds(p * here, here)], fac_send, fac_recv, rows
     )
     start()
+    ask = pair(wish_out, wish_in, 2, {"groups": 1 - group})
+    ask.start()
     forward()
-
-    half_out[...] = fac[wanted[1]]
-    swap = pltpu.make_async_remote_copy(
-        src_ref=half_out,
-        dst_ref=half_in,
-        send_sem=pair_send.at[0],
-        recv_sem=pair_recv.at[0],
-        device_id={"groups": 1 - group},
-        device_id_type=MESH,
-    )
-    swap.start()
-    own = fac[wanted[0]]
+    ask.wait_recv()
+    note = pltpu.make_async_copy(wish_in, wish, local.at[4])
+    note.start()
+    note.wait()
     for load in loads:
         load.wait()
+    beside()
+
+    half_out[...] = fac[wish[0, 0]]
+    swap = pair(half_out, half_in, 0, {"groups": 1 - group})
+    swap.start()
+
+    def dot(a, b, dims=(((1,), (0,)), ((), ()))):
+        return lax.dot_general(a, b, dims, preferred_element_type=jnp.float32)
+
+    def part(index, width):
+        return pl.ds(pl.multiple_of(index * width, 128), width)
+
+    own = fac[slot]
+    own_down = dot(own[:, :ih], act[:, part(group, ih)], NT)
+    own_up = dot(own[:, ih:], cot[:, part(group, hh)], NT)
     swap.wait_recv()
     other = half_in[...]
-    first = group == 0
-    left = jnp.where(first, own, other)
-    right = jnp.where(first, other, own)
-
-    def dot(a, b, dims=(((1,), (0,)), ((), ()))):
-        return lax.dot_general(a, b, dims, preferred_element_type=jnp.float32)
-
-    rank = left.shape[0]
-    sum_out[0:rank] = dot(left[:, :ih], act[:, :ih], NT) + dot(right[:, :ih], act[:, ih:], NT)
-    sum_out[rank:] = dot(left[:, ih:], cot[:, :hh], NT) + dot(right[:, ih:], cot[:, hh:], NT)
-    pair = pltpu.make_async_remote_copy(
-        src_ref=sum_out,
-        dst_ref=sum_in,
-        send_sem=pair_send.at[1],
-        recv_sem=pair_recv.at[1],
-        device_id={"tp": 1 - core},
-        device_id_type=MESH,
-    )
-    pair.start()
-    pair.wait_recv()
+    sum_out[0:rank] = own_down + dot(other[:, :ih], act[:, part(1 - group, ih)], NT)
+    sum_out[rank:] = own_up + dot(other[:, ih:], cot[:, part(1 - group, hh)], NT)
+    share = pair(sum_out, sum_in, 1, {"tp": 1 - core})
+    share.start()
+    share.wait_recv()
     sums = sum_out[...] + sum_in[...]
-    low_down = (live[...] * sums[:rank]).astype(jnp.bfloat16)
-    low_up = (adapter_scale * live[...] * sums[rank:]).astype(jnp.bfloat16)
+    low_down = (live * sums[:rank]).astype(jnp.bfloat16)
+    low_up = (adapter_scale * live * sums[rank:]).astype(jnp.bfloat16)
 
     terms[me, :, 0:inputs] = dot(low_up, act[...]).astype(jnp.bfloat16)
     terms[me, :, inputs:] = (adapter_scale * dot(low_down, cot[...])).astype(jnp.bfloat16)
-    start2, forward2, drain2 = line_gather(
+    start2, forward2, beside2, drain2 = line_gather(
         terms, lambda r, p: r.at[p], term_send, term_recv, rows
     )
     start2()
-    input_grad[:, 0:ih] = dot(low_up, left[:, :ih], TN).astype(jnp.bfloat16)
-    input_grad[:, ih:] = dot(low_up, right[:, :ih], TN).astype(jnp.bfloat16)
+    input_grad[:, part(group, ih)] = dot(low_up, own[:, :ih], TN).astype(jnp.bfloat16)
+    input_grad[:, part(1 - group, ih)] = dot(low_up, other[:, :ih], TN).astype(jnp.bfloat16)
+    drain()
     forward2()
 
     tile = 512
+
+    def weights(which):
+        slots = [slot_of[block_adapter[z * LANES + which]] for z in range(line)]
+        return [
+            [jnp.where(s == me * here + j, 1.0, 0.0) for s in slots] for j in range(here)
+        ]
+
+    def add(which, mask, source, j):
+        total = mask[j][0] * terms[which, :, source].astype(jnp.float32)
+        for z in range(1, line):
+            total += mask[j][z] * terms[z * LANES + which, :, source].astype(jnp.float32)
+        return total
+
+    same_lane = weights(lane)
+
+    def first(i, carry):
+        source = part(i, tile)
+        for j in range(here):
+            totals[j, :, source] = add(lane, same_lane, source, j)
+        return carry
+
+    lax.fori_loop(0, (inputs + hidden) // tile, first, 0)
+    beside2()
+    other_lane = weights(1 - lane)
     for out, base, width in ((grad_down, 0, inputs), (grad_up, inputs, hidden)):
 
-        def add(i, carry, out=out, base=base):
-            to = pl.ds(pl.multiple_of(i * tile, tile), tile)
+        def second(i, carry, out=out, base=base):
             source = pl.ds(pl.multiple_of(base + i * tile, tile), tile)
-            totals = [jnp.zeros((rank, tile), jnp.float32) for _ in range(here)]
-            for b in range(rows):
-                term = terms[b, :, source].astype(jnp.float32)
-                for j in range(here):
-                    mask = jnp.where(block_slots[b] == me * here + j, 1.0, 0.0)
-                    totals[j] += mask * term
             for j in range(here):
-                out[j, :, to] = totals[j].astype(jnp.bfloat16)
+                total = totals[j, :, source] + add(1 - lane, other_lane, source, j)
+                out[j, :, part(i, tile)] = total.astype(jnp.bfloat16)
             return carry
 
-        lax.fori_loop(0, width // tile, add, 0)
-
-    drain()
+        lax.fori_loop(0, width // tile, second, 0)
+
     drain2()
+    ask.wait_send()
     swap.wait_send()
-    pair.wait_send()
+    share.wait_send()
 
 
 def tenant_plan(
@@ -334,27 +388,11 @@
     adapter_of_block,
     counts,
 ):
-    active_rows, slot_of_block = row_plan(adapter_of_block, counts, adapter_slot)
     rows = jax.lax.axis_size("rows")
-    me = lax.axis_index("rows")
-    group = lax.axis_index("groups")
     here, inputs, rank = adapter_down_factors.shape
     hidden = adapter_up_factors.shape[1]
     half = (inputs + hidden) // 2
-    down = jnp.swapaxes(adapter_down_factors, 1, 2)
-    up = jnp.swapaxes(adapter_up_factors, 1, 2)
-    mine = jnp.concatenate(
-        [
-            lax.dynamic_slice_in_dim(down, group * (inputs // 2), inputs // 2, 2),
-            lax.dynamic_slice_in_dim(up, group * (hidden // 2), hidden // 2, 2),
-        ],
-        axis=2,
-    )
-    slot = slot_of_block[me]
-    both = lax.all_gather(slot_of_block, "groups")
-    wanted = jnp.stack([slot, both[1 - group, me]])
-    live = lax.dynamic_slice_in_dim(active_rows, me, 1, 0)
-    bf16, f32 = jnp.bfloat16, jnp.float32
+    bf16, f32, i32 = jnp.bfloat16, jnp.float32, jnp.int32
     line = rows // LANES
     vmem = pl.BlockSpec(memory_space=pltpu.VMEM)
     smem = pl.BlockSpec(memory_space=pltpu.SMEM)
@@ -367,29 +405,41 @@
             jax.ShapeDtypeStruct((here, rank, inputs), bf16),
             jax.ShapeDtypeStruct((here, rank, hidden), bf16),
         ),
-        in_specs=[smem, smem, vmem, vmem, hbm, hbm],
+        in_specs=[smem, smem, smem, hbm, hbm, hbm, hbm],
         out_specs=(vmem, vmem, vmem),
         scratch_shapes=[
             pltpu.VMEM((rows * here, rank, half), bf16),
             pltpu.VMEM((rows, rank, inputs + hidden), bf16),
+            pltpu.VMEM((here, rank, inputs + hidden), f32),
             pltpu.VMEM((BLK, inputs), bf16),
             pltpu.VMEM((BLK, hidden), bf16),
             pltpu.VMEM((rank, half), bf16),
             pltpu.VMEM((rank, half), bf16),
             pltpu.VMEM((2 * rank, BLK), f32),
             pltpu.VMEM((2 * rank, BLK), f32),
+            pltpu.VMEM((8, 128), i32),
+            pltpu.VMEM((8, 128), i32),
+            pltpu.SMEM((8, 128), i32),
             dma((3, line)),
             dma((rows,)),
             dma((3, line)),
             dma((rows,)),
-            dma((2,)),
-            dma((2,)),
-            dma((2,)),
+            dma((3,)),
+            dma((3,)),
+            dma((5,)),
         ],
         compiler_params=pltpu.CompilerParams(
             collective_id=0, has_side_effects=True, vmem_limit_bytes=40 << 20
         ),
-    )(wanted, slot_of_block, live, mine, activations, cotangent)
+    )(
+        adapter_slot,
+        adapter_of_block,
+        counts,
+        jnp.swapaxes(adapter_down_factors, 1, 2),
+        jnp.swapaxes(adapter_up_factors, 1, 2),
+        activations,
+        cotangent,
+    )
     return input_grad, jnp.swapaxes(grad_down, 1, 2), jnp.swapaxes(grad_up, 1, 2)
 
 

time: 95.5 us -> 87.9 us (0.920)
  blocking collectives: 5.22 us -> 0 us
  other arithmetic: 3.28 us -> 0 us
  Pallas kernels: 76.8 us -> 78.2 us
    unnamed x1 -> x0, blocking collectives: 5.22 us -> none
    unnamed x12 -> x17, local copies, waits for them, and re-layouts: 6.37 us -> 8.78 us
    dynamic_slice x5 -> x0, local copies, waits for them, and re-layouts: 2.05 us -> none  [the longest x1 0.85 us: tenant_plan(): lax.dynamic_slice_in_dim(down, group * (inputs // 2), inputs // 2, 2)]
    reduce_sum x2 -> x0, other arithmetic: 1.81 us -> none  [the longest x1 0.91 us: row_plan(): jnp.sum(jnp.where(same_adapter & (order[None, :] < order[:, None]), 1, 0)...]
    pallas_call x1, Pallas kernels: 76.8 us -> 78.2 us  [tenant_plan(): pl.pallas_call(functools.partial(tenant_kernel, rows), out_shape=(jax.Sha...]
    another operation x1 -> x0, other arithmetic: 1.37 us -> none  [tenant_plan(): wanted = jnp.stack([slot, both[1 - group, me]])]
where the time goes in v3:
time: 87.9 us; the launch traced here: 87.6 us
  Pallas kernels  78.2 us (89%)
  local copies, waits for them, and re-layouts  8.78 us (10%)
    pallas_call x1, Pallas kernels, tenant_plan(): pl.pallas_call(functools.partial(tenant_kernel, rows), out_shape=(jax.Sha...  78.2 us
    unnamed x17, local copies, waits for them, and re-layouts  8.78 us

profile of v3, /device:TPU:0, one launch (start us, length us, event | category | flops | bytes accessed | tf_op | source)
XLA Modules:
  0.0 87.6 jit_solution(12121097286477712775)
XLA Ops:
  0.6 0.0 copy-start
  0.6 1.6 %copy-done = bf16[128,8192]{1,0:T(8,128)(2,1)S(1)} copy-done((bf16[128,8192]{1,0:T(8,128)(2,1)S(1)}, bf16[128,8192]{1,0:T(8,128)(2,1)}, u32[]{:S(2)}) %copy-start) | copy-done | bytes 2097176
  2.2 0.0 copy-start.1
  2.2 1.0 %copy-done.1 = bf16[2,8192,16]{1,2,0:T(8,128)(2,1)S(1)} copy-done((bf16[2,8192,16]{1,2,0:T(8,128)(2,1)S(1)}, bf16[2,8192,16]{1,2,0:T(8,128)(2,1)}, u32[]{:S(2)}) %copy-start.1) | copy-done | bytes 524312
  3.3 0.0 copy-start.2
  3.3 1.0 %copy-done.2 = bf16[128,2048]{1,0:T(8,128)(2,1)S(1)} copy-done((bf16[128,2048]{1,0:T(8,128)(2,1)S(1)}, bf16[128,2048]{1,0:T(8,128)(2,1)}, u32[]{:S(2)}) %copy-start.2) | copy-done | bytes 524312
  4.3 0.0 copy-start.3
  4.3 0.9 %copy-done.3 = bf16[2,2048,16]{1,2,0:T(8,128)(2,1)S(1)} copy-done((bf16[2,2048,16]{1,2,0:T(8,128)(2,1)S(1)}, bf16[2,2048,16]{1,2,0:T(8,128)(2,1)}, u32[]{:S(2)}) %copy-start.3) | copy-done | bytes 131096
  5.2 0.0 copy-start.4
  5.2 0.7 copy-done.4
  5.9 0.0 copy-start.5
  5.9 0.7 copy-done.5
  6.5 0.0 copy-start.6
  6.5 0.7 copy-done.6
  7.2 78.2 %shard_map.94 = (bf16[128,2048]{1,0:T(8,128)(2,1)S(1)}, bf16[2,16,2048]{2,1,0:T(8,128)(2,1)S(1)}, bf16[2,16,8192]{2,1,0:T(8,128)(2,1)S(1)}) custom-call(s32[16]{0:T(128)S(1)} %copy-done.4, s32[8]{0:T(128)S(1)} %copy-done.5, s32[16]{0:T(128)S(1)} %copy-done.6, bf16[2,16,2048]{2,1,0:T(8,128)(2,1)S(1)} %bitcast.6, bf16[2,16,8192]{2,1,0:T(8,128)(2,1)S(1)} %bitcast.4, ...), custom_call_target="tpu_custom_call" | custom-call | tf_op jit(solution)/shard_map/pallas_call | solution.py:401
  85.4 0.8 copy.13
  86.2 0.7 copy.14
  86.9 0.8 copy.15
Async XLA Ops:
  0.6 1.6 %copy-start = (bf16[128,8192]{1,0:T(8,128)(2,1)S(1)}, bf16[128,8192]{1,0:T(8,128)(2,1)}, u32[]{:S(2)}) copy-start(bf16[128,8192]{1,0:T(8,128)(2,1)} %cot_hbm.1) | copy-start | bytes 6291460
  2.2 1.0 %copy-start.1 = (bf16[2,8192,16]{1,2,0:T(8,128)(2,1)S(1)}, bf16[2,8192,16]{1,2,0:T(8,128)(2,1)}, u32[]{:S(2)}) copy-start(bf16[2,8192,16]{1,2,0:T(8,128)(2,1)} %param.10) | copy-start | bytes 1572868
  3.3 1.0 %copy-start.2 = (bf16[128,2048]{1,0:T(8,128)(2,1)S(1)}, bf16[128,2048]{1,0:T(8,128)(2,1)}, u32[]{:S(2)}) copy-start(bf16[128,2048]{1,0:T(8,128)(2,1)} %act_hbm.1) | copy-start | bytes 1572868
  4.3 0.9 %copy-start.3 = (bf16[2,2048,16]{1,2,0:T(8,128)(2,1)S(1)}, bf16[2,2048,16]{1,2,0:T(8,128)(2,1)}, u32[]{:S(2)}) copy-start(bf16[2,2048,16]{1,2,0:T(8,128)(2,1)} %param.9) | copy-start | bytes 393220
  5.2 0.7 copy-start.4
  5.9 0.7 copy-start.5
  6.5 0.7 copy-start.6

commit v4 on v3

--- a/solution.py
+++ b/solution.py
@@ -103,12 +103,13 @@
 
 
 LANES = 2
+CHUNKS = 2
 MESH = pl.DeviceIdType.MESH
 NT = (((1,), (1,)), ((), ()))
 TN = (((0,), (0,)), ((), ()))
 
 
-def line_gather(buf, piece, send, recv, rows):
+def line_gather(buf, piece, send, recv, rows, chunk=0, hand=True):
     line = rows // LANES
     me = lax.axis_index("rows")
     at, lane = me // LANES, me % LANES
@@ -117,8 +118,8 @@
         return pltpu.make_async_remote_copy(
             src_ref=piece(buf, p),
             dst_ref=piece(buf, p),
-            send_sem=send.at[where, p // LANES],
-            recv_sem=recv.at[p],
+            send_sem=send.at[3 * chunk + where, p // LANES],
+            recv_sem=recv.at[rows * chunk + p],
             device_id={"rows": to},
             device_id_type=MESH,
         )
@@ -135,7 +136,8 @@
         def _():
             copy(1, me, me - LANES).start()
 
-        copy(2, me, me ^ 1).start()
+        if hand:
+            copy(2, me, me ^ 1).start()
 
     def forward():
         for k in range(1, line):
@@ -149,7 +151,8 @@
                 def _():
                     copy(0, low, me + LANES).start()
 
-                copy(2, low, me ^ 1).start()
+                if hand:
+                    copy(2, low, me ^ 1).start()
 
             @pl.when(at + k < line)
             def _():
@@ -159,7 +162,8 @@
                 def _():
                     copy(1, high, me - LANES).start()
 
-                copy(2, high, me ^ 1).start()
+                if hand:
+                    copy(2, high, me ^ 1).start()
 
     def beside():
         for z in range(line):
@@ -168,7 +172,8 @@
     def drain():
         for z in range(line):
             p = z * LANES + lane
-            copy(2, p, me ^ 1).wait_send()
+            if hand:
+                copy(2, p, me ^ 1).wait_send()
 
             @pl.when(jnp.logical_and(z <= at, at < line - 1))
             def _():
@@ -193,13 +198,17 @@
     input_grad,
     grad_down,
     grad_up,
-    fac,
+    fac_low,
+    fac_high,
     terms,
     totals,
     act,
     cot,
     half_out,
     half_in,
+    own_half,
+    beside_out,
+    beside_in,
     sum_out,
     sum_in,
     wish_out,
@@ -221,18 +230,26 @@
     here, rank, inputs = grad_down.shape
     hidden = cot.shape[1]
     ih, hh = inputs // 2, hidden // 2
-    spot = pl.ds(me * here, here)
-
+    spot = pl.ds(at * here, here)
+
+    fac = (fac_low, fac_high)
+    width = fac_low.shape[2]
+    up_low, up_high = width - ih, width
     own_factors = [
         pltpu.make_async_copy(
             down_hbm.at[:, :, pl.ds(pl.multiple_of(group * ih, 128), ih)],
-            fac.at[spot, :, pl.ds(0, ih)],
+            fac_low.at[spot, :, pl.ds(0, ih)],
             local.at[2],
         ),
         pltpu.make_async_copy(
-            up_hbm.at[:, :, pl.ds(pl.multiple_of(group * hh, 128), hh)],
-            fac.at[spot, :, pl.ds(ih, hh)],
+            up_hbm.at[:, :, pl.ds(pl.multiple_of(group * hh, 128), up_low)],
+            fac_low.at[spot, :, pl.ds(ih, up_low)],
             local.at[3],
+        ),
+        pltpu.make_async_copy(
+            up_hbm.at[:, :, pl.ds(pl.multiple_of(group * hh + up_low, 128), up_high)],
+            fac_high.at[spot],
+            local.at[5],
         ),
     ]
     for load in own_factors:
@@ -269,7 +286,9 @@
         earlier += jnp.where(same, 1, 0)
     place = lax.broadcasted_iota(jnp.int32, (1, BLK), 1)
     live = jnp.where(earlier * BLK + place < counts[adapter], 1.0, 0.0)
-    wish_out[...] = jnp.full(wish_out.shape, slot, jnp.int32)
+    slot_beside = slot_of[block_adapter[me ^ 1]]
+    row = lax.broadcasted_iota(jnp.int32, wish_out.shape, 0)
+    wish_out[...] = jnp.where(row == 0, slot, slot_beside)
 
     for load in own_factors:
         load.wait()
@@ -287,24 +306,64 @@
             device_id_type=MESH,
         )
 
-    start, forward, beside, drain = line_gather(
-        fac, lambda r, p: r.at[pl.ds(p * here, here)], fac_send, fac_recv, rows
-    )
-    start()
+    chunks = [pl.ds(c * width, width) for c in range(CHUNKS)]
+    gathers = [
+        line_gather(
+            fac[c],
+            lambda r, p: r.at[pl.ds((p // LANES) * here, here)],
+            fac_send,
+            fac_recv,
+            rows,
+            chunk=c,
+            hand=False,
+        )
+        for c in range(CHUNKS)
+    ]
+
+    def place_of(s):
+        owner = s // here
+        return (owner // LANES) * here + s % here, owner % LANES == lane
+
     ask = pair(wish_out, wish_in, 2, {"groups": 1 - group})
-    ask.start()
-    forward()
-    ask.wait_recv()
-    note = pltpu.make_async_copy(wish_in, wish, local.at[4])
-    note.start()
-    note.wait()
+    hands, swaps = [], []
+
+    def hand_over(c):
+        beside_out[c, 0] = fac[c][place_of(slot_beside)[0]]
+        beside_out[c, 1] = fac[c][place_of(wish[1, 0])[0]]
+        hands.append(pair(beside_out.at[c], beside_in.at[c], 3 + c, {"rows": me ^ 1}))
+        hands[c].start()
+
+    def swap_over(c):
+        cols = chunks[c]
+        hands[c].wait_recv()
+        where, local_lane = place_of(wish[0, 0])
+        half_out[c] = jnp.where(local_lane, fac[c][where], beside_in[c, 1])
+        swaps.append(
+            pair(half_out.at[c], half_in.at[c], 3 + CHUNKS + c, {"groups": 1 - group})
+        )
+        swaps[c].start()
+        where, local_lane = place_of(slot)
+        own_half[:, cols] = jnp.where(local_lane, fac[c][where], beside_in[c, 0])
+
+    for c in range(CHUNKS):
+        start, forward, _, _ = gathers[c]
+        start()
+        if c == 0:
+            ask.start()
+        else:
+            hand_over(c - 1)
+        forward()
+        if c == 0:
+            ask.wait_recv()
+            note = pltpu.make_async_copy(wish_in, wish, local.at[4])
+            note.start()
+            note.wait()
+        else:
+            swap_over(c - 1)
+    hand_over(CHUNKS - 1)
     for load in loads:
         load.wait()
-    beside()
-
-    half_out[...] = fac[wish[0, 0]]
-    swap = pair(half_out, half_in, 0, {"groups": 1 - group})
-    swap.start()
+    swap_over(CHUNKS - 1)
 
     def dot(a, b, dims=(((1,), (0,)), ((), ()))):
         return lax.dot_general(a, b, dims, preferred_element_type=jnp.float32)
@@ -312,11 +371,12 @@
     def part(index, width):
         return pl.ds(pl.multiple_of(index * width, 128), width)
 
-    own = fac[slot]
+    own = own_half[...]
     own_down = dot(own[:, :ih], act[:, part(group, ih)], NT)
     own_up = dot(own[:, ih:], cot[:, part(group, hh)], NT)
-    swap.wait_recv()
-    other = half_in[...]
+    for swap in swaps:
+        swap.wait_recv()
+    other = jnp.concatenate([half_in[c] for c in range(CHUNKS)], axis=1)
     sum_out[0:rank] = own_down + dot(other[:, :ih], act[:, part(1 - group, ih)], NT)
     sum_out[rank:] = own_up + dot(other[:, ih:], cot[:, part(1 - group, hh)], NT)
     share = pair(sum_out, sum_in, 1, {"tp": 1 - core})
@@ -334,7 +394,8 @@
     start2()
     input_grad[:, part(group, ih)] = dot(low_up, own[:, :ih], TN).astype(jnp.bfloat16)
     input_grad[:, part(1 - group, ih)] = dot(low_up, other[:, :ih], TN).astype(jnp.bfloat16)
-    drain()
+    for gather in gathers:
+        gather[3]()
     forward2()
 
     tile = 512
@@ -375,7 +436,9 @@
 
     drain2()
     ask.wait_send()
-    swap.wait_send()
+    for c in range(CHUNKS):
+        hands[c].wait_send()
+        swaps[c].wait_send()
     share.wait_send()
 
 
@@ -408,25 +471,29 @@
         in_specs=[smem, smem, smem, hbm, hbm, hbm, hbm],
         out_specs=(vmem, vmem, vmem),
         scratch_shapes=[
-            pltpu.VMEM((rows * here, rank, half), bf16),
+            pltpu.VMEM((line * here, rank, half // CHUNKS), bf16),
+            pltpu.VMEM((line * here, rank, half // CHUNKS), bf16),
             pltpu.VMEM((rows, rank, inputs + hidden), bf16),
             pltpu.VMEM((here, rank, inputs + hidden), f32),
             pltpu.VMEM((BLK, inputs), bf16),
             pltpu.VMEM((BLK, hidden), bf16),
+            pltpu.VMEM((CHUNKS, rank, half // CHUNKS), bf16),
+            pltpu.VMEM((CHUNKS, rank, half // CHUNKS), bf16),
             pltpu.VMEM((rank, half), bf16),
-            pltpu.VMEM((rank, half), bf16),
+            pltpu.VMEM((CHUNKS, 2, rank, half // CHUNKS), bf16),
+            pltpu.VMEM((CHUNKS, 2, rank, half // CHUNKS), bf16),
             pltpu.VMEM((2 * rank, BLK), f32),
             pltpu.VMEM((2 * rank, BLK), f32),
             pltpu.VMEM((8, 128), i32),
             pltpu.VMEM((8, 128), i32),
             pltpu.SMEM((8, 128), i32),
+            dma((3 * CHUNKS, line)),
+            dma((rows * CHUNKS,)),
             dma((3, line)),
             dma((rows,)),
-            dma((3, line)),
-            dma((rows,)),
-            dma((3,)),
-            dma((3,)),
-            dma((5,)),
+            dma((3 + 2 * CHUNKS,)),
+            dma((3 + 2 * CHUNKS,)),
+            dma((6,)),
         ],
         compiler_params=pltpu.CompilerParams(
             collective_id=0, has_side_effects=True, vmem_limit_bytes=40 << 20

time: 87.9 us -> 90.7 us (1.032)
  Pallas kernels: 78.2 us -> 81 us
    pallas_call x1, Pallas kernels: 78.2 us -> 81 us  [tenant_plan(): pl.pallas_call(functools.partial(tenant_kernel, rows), out_shape=(jax.Sha...]
where the time goes in v4:
time: 90.7 us; the launch traced here: 90.5 us
  Pallas kernels  81 us (89%)
  local copies, waits for them, and re-layouts  8.78 us (10%)
    pallas_call x1, Pallas kernels, tenant_plan(): pl.pallas_call(functools.partial(tenant_kernel, rows), out_shape=(jax.Sha...  81 us
    unnamed x17, local copies, waits for them, and re-layouts  8.78 us

profile of v4, /device:TPU:0, one launch (start us, length us, event | category | flops | bytes accessed | tf_op | source)
XLA Modules:
  0.0 90.5 jit_solution(11307216889895976007)
XLA Ops:
  0.6 0.0 copy-start
  0.6 1.6 %copy-done = bf16[128,8192]{1,0:T(8,128)(2,1)S(1)} copy-done((bf16[128,8192]{1,0:T(8,128)(2,1)S(1)}, bf16[128,8192]{1,0:T(8,128)(2,1)}, u32[]{:S(2)}) %copy-start) | copy-done | bytes 2097176
  2.2 0.0 copy-start.1
  2.2 1.0 %copy-done.1 = bf16[2,8192,16]{1,2,0:T(8,128)(2,1)S(1)} copy-done((bf16[2,8192,16]{1,2,0:T(8,128)(2,1)S(1)}, bf16[2,8192,16]{1,2,0:T(8,128)(2,1)}, u32[]{:S(2)}) %copy-start.1) | copy-done | bytes 524312
  3.3 0.0 copy-start.2
  3.3 1.0 %copy-done.2 = bf16[128,2048]{1,0:T(8,128)(2,1)S(1)} copy-done((bf16[128,2048]{1,0:T(8,128)(2,1)S(1)}, bf16[128,2048]{1,0:T(8,128)(2,1)}, u32[]{:S(2)}) %copy-start.2) | copy-done | bytes 524312
  4.3 0.0 copy-start.3
  4.3 0.9 copy-done.3
  5.2 0.0 copy-start.4
  5.2 0.7 copy-done.4
  5.9 0.0 copy-start.5
  5.9 0.7 copy-done.5
  6.5 0.0 copy-start.6
  6.5 0.7 copy-done.6
  7.2 81.0 %shard_map.94 = (bf16[128,2048]{1,0:T(8,128)(2,1)S(1)}, bf16[2,16,2048]{2,1,0:T(8,128)(2,1)S(1)}, bf16[2,16,8192]{2,1,0:T(8,128)(2,1)S(1)}) custom-call(s32[16]{0:T(128)S(1)} %copy-done.4, s32[8]{0:T(128)S(1)} %copy-done.5, s32[16]{0:T(128)S(1)} %copy-done.6, bf16[2,16,2048]{2,1,0:T(8,128)(2,1)S(1)} %bitcast.6, bf16[2,16,8192]{2,1,0:T(8,128)(2,1)S(1)} %bitcast.4, ...), custom_call_target="tpu_custom_call" | custom-call | tf_op jit(solution)/shard_map/pallas_call | solution.py:464
  88.2 0.8 copy.13
  89.0 0.7 copy.14
  89.7 0.8 copy.15
Async XLA Ops:
  0.6 1.6 %copy-start = (bf16[128,8192]{1,0:T(8,128)(2,1)S(1)}, bf16[128,8192]{1,0:T(8,128)(2,1)}, u32[]{:S(2)}) copy-start(bf16[128,8192]{1,0:T(8,128)(2,1)} %cot_hbm.1) | copy-start | bytes 6291460
  2.2 1.0 %copy-start.1 = (bf16[2,8192,16]{1,2,0:T(8,128)(2,1)S(1)}, bf16[2,8192,16]{1,2,0:T(8,128)(2,1)}, u32[]{:S(2)}) copy-start(bf16[2,8192,16]{1,2,0:T(8,128)(2,1)} %param.10) | copy-start | bytes 1572868
  3.3 1.0 %copy-start.2 = (bf16[128,2048]{1,0:T(8,128)(2,1)S(1)}, bf16[128,2048]{1,0:T(8,128)(2,1)}, u32[]{:S(2)}) copy-start(bf16[128,2048]{1,0:T(8,128)(2,1)} %act_hbm.1) | copy-start | bytes 1572868
  4.3 0.9 copy-start.3
  5.2 0.7 copy-start.4
  5.9 0.7 copy-start.5
  6.5 0.7 copy-start.6

commit v5 on v3

--- a/solution.py
+++ b/solution.py
@@ -429,7 +429,7 @@
             dma((5,)),
         ],
         compiler_params=pltpu.CompilerParams(
-            collective_id=0, has_side_effects=True, vmem_limit_bytes=40 << 20
+            collective_id=0, has_side_effects=True, vmem_limit_bytes=60 << 20
         ),
     )(
         adapter_slot,

time: 87.9 us -> 85.4 us (0.972)
  local copies, waits for them, and re-layouts: 8.78 us -> 5.32 us
  Pallas kernels: 78.2 us -> 79.2 us
    unnamed x17 -> x3, local copies, waits for them, and re-layouts: 8.78 us -> 5.32 us
    pallas_call x1, Pallas kernels: 78.2 us -> 79.2 us  [tenant_plan(): pl.pallas_call(functools.partial(tenant_kernel, rows), out_shape=(jax.Sha...]
where the time goes in v5:
time: 85.4 us; the launch traced here: 85.1 us
  Pallas kernels  79.2 us (93%)
  local copies, waits for them, and re-layouts  5.32 us (6%)
    pallas_call x1, Pallas kernels, tenant_plan(): pl.pallas_call(functools.partial(tenant_kernel, rows), out_shape=(jax.Sha...  79.2 us
    unnamed x3, local copies, waits for them, and re-layouts  5.32 us

profile of v5, /device:TPU:0, one launch (start us, length us, event | category | flops | bytes accessed | tf_op | source)
XLA Modules:
  0.0 85.1 jit_solution(1164785176007415245)
XLA Ops:
  0.6 79.2 %shard_map.94 = (bf16[128,2048]{1,0:T(8,128)(2,1)}, bf16[2,16,2048]{2,1,0:T(8,128)(2,1)}, bf16[2,16,8192]{2,1,0:T(8,128)(2,1)}) custom-call(s32[16]{0:T(128)} %slot_of.1, s32[8]{0:T(128)} %block_adapter.1, s32[16]{0:T(128)} %counts.1, bf16[2,16,2048]{2,1,0:T(8,128)(2,1)} %bitcast.6, bf16[2,16,8192]{2,1,0:T(8,128)(2,1)} %bitcast.4, ...), custom_call_target="tpu_custom_call" | custom-call | tf_op jit(solution)/shard_map/pallas_call | solution.py:401
  79.8 1.9 %copy.13 = bf16[128,2048]{1,0:T(8,128)(2,1)} copy(bf16[128,2048]{1,0:T(8,128)(2,1)} %get-tuple-element.12) | data formatting | bytes 1048576
  81.7 1.6 %copy.14 = bf16[2,2048,16]{1,2,0:T(8,128)(2,1)} copy(bf16[2,2048,16]{1,2,0:T(8,128)(2,1)} %bitcast.7) | data formatting | bytes 262144
  83.3 1.9 %copy.15 = bf16[2,8192,16]{1,2,0:T(8,128)(2,1)} copy(bf16[2,8192,16]{1,2,0:T(8,128)(2,1)} %bitcast.5) | data formatting | bytes 1048576
